TPU v7x, 128 devices: a whole 4x4x4 slice. The times are simulated.
128 devices in a mesh: dp: 32 (over z, y, core), ctx: 4 (over x).
Axes of the slice: x: 4, y: 4, z: 4, core: 2. Of those that a mesh axis runs over, the one named last changes fastest.
Arguments:
- q_rows: bfloat16 [16384, 8192], P(('dp', 'ctx')), may hold values from -6 to 6
- k_rows: bfloat16 [16384, 8192], P(('dp', 'ctx')), may hold values from -6 to 6
- v_rows: bfloat16 [16384, 8192], P(('dp', 'ctx')), may hold values from -6 to 6
- out_grad: bfloat16 [16384, 8192], P(('dp', 'ctx')), may hold values from -24 to 24
- filters: float32 [512, 128], replicated, may hold values from -0.5 to 0.5
- skip_gain: float32 [8192], replicated, may hold values from -4 to 4
- genome_len: int32 [32, 3], P('dp'), may hold values from 1 to 256, 512 in all within a row
- plan_offset: int32 [128, 128, 1], P(None, ('dp', 'ctx')), may hold values from 0 to 127, as said below
Outputs:
- mixer_out: bfloat16 [16384, 8192], P(('dp', 'ctx'))
- q_grad: bfloat16 [16384, 8192], P(('dp', 'ctx'))
- k_grad: bfloat16 [16384, 8192], P(('dp', 'ctx'))
- v_grad: bfloat16 [16384, 8192], P(('dp', 'ctx'))
- filter_grad: float32 [512, 128], P(('dp', 'ctx'))
- skip_grad: float32 [8192], P(('dp', 'ctx'))
Inputs may be any that keep to these rules, and one draw needn't show every extreme that they name: For every member b, the values plan_offset[a, b, c] over all loaders a and slots c are each of 0 to 127 exactly once, and each loader's slots for b are one run of 1 row, plan_offset[a, b, c] = plan_offset[a, b, 0] + c, starting at a multiple of 1.
All inputs are finite; a program needn't handle non-finite values.
Results may differ from a plain program's by a relative error of at most 0.0056.
Values may be sent and summed in bfloat16 or wider, within the bound.
A program may use at most 320 MiB of HBM per device.

v0:
```python
import math

import jax
import jax.numpy as jnp
from jax import lax
from jax.experimental import pallas as pl
from jax.experimental.pallas import tpu as pltpu
from jax.sharding import PartitionSpec as P

BF = jnp.bfloat16
F32 = jnp.float32
I32 = jnp.int32
MESH = pl.DeviceIdType.MESH
T = 128
NCH = 8
LB = 8
WIDE = LB * T
GRID = (4, 4, 2, 4)
PREP, PLAN, CONV, LAST, MOVE_THERE, MOVE_BACK, MOVE_TERMS = range(7)
ORDERS_THERE = ("xzy", "yxz", "yzx", "xyz", "xzy", "xyz", "yxz", "yxz")
ORDERS_BACK = ("zyx", "zxy", "zxy", "zyx", "yzx", "zyx", "zxy", "zyx")
SCHEDULE = (
    0, 400, 0, 410, 0, 420, 0, 430, 401, 411, 0, 440, 0, 450, 421, 431, 402, 0, 460, 412, 422,
    441, 432, 451, 403, 100, 442, 0, 470, 461, 413, 100, 423, 100, 452, 200, 500, 433, 100, 471,
    443, 100, 200, 510, 501, 453, 100, 462, 200, 520, 200, 530, 463, 100, 472, 502, 200, 540, 521,
    200, 550, 531, 473, 100, 200, 560, 511, 551, 532, 522, 541, 200, 570, 600, 561, 503, 300, 601,
    512, 552, 602, 542, 571, 603, 513, 300, 523, 300, 533, 300, 562, 572, 543, 300, 553, 300, 563,
    300, 573, 300,
)


def dot(a, b, dims=((1,), (0,))):
    return lax.dot_general(a, b, (dims, ((), ())), preferred_element_type=F32)


def iota(axis, shape=(T, T)):
    return lax.broadcasted_iota(I32, shape, axis)


def lanes(r):
    return slice(r * T, (r + 1) * T)


def mixer_kernel(
    q_hbm, k_hbm, v_hbm, g_hbm, taps_ref, gain_ref, len_ref, off_ref,
    out_hbm, qg_hbm, kg_hbm, vg_hbm, sum_ref,
    qv, kv, vv, gv, fa, fb, fc, fd, ba, bb, bc, bd, qp, up, ear, inn, lat,
    wmask, vmask, hmask, place, fetch, taps, rtaps, w_sc, v_sc, sc, dq_sc, du_sc,
    term, rx, ry, rz, s1, s2,
    in_sem, out_sem, fs, fr, fl, bs, br, bl, hs, hr, rs, rr,
):
    dp = lax.axis_index("dp")
    cx = lax.axis_index("ctx")
    z, y, k = dp // 8, lax.rem(dp // 2, 4), lax.rem(dp, 2)
    me = (dp, cx)
    peers = {
        "x": [(dp, lax.rem(cx + i, 4)) for i in (1, 3, 2)],
        "y": [(z * 8 + lax.rem(y + i, 4) * 2 + k, cx) for i in (1, 3, 2)],
        "z": [
            (lax.rem(z + i, 4) * 8 + y * 2 + lax.rem(k + j, 2), cx)
            for i, j in ((1, 0), (3, 0), (2, 0), (1, 1), (3, 1), (2, 1), (0, 1))
        ],
    }
    barrier = pltpu.get_barrier_semaphore()
    for axis in "xyz":
        for peer in peers[axis]:
            pl.semaphore_signal(barrier, inc=1, device_id=peer, device_id_type=MESH)

    pairs_in = ((q_hbm, qv), (k_hbm, kv), (v_hbm, vv), (g_hbm, gv))

    def cols(c):
        return pl.ds(pl.multiple_of(c * WIDE, WIDE), WIDE)

    def block_of(c, r):
        return pl.ds(pl.multiple_of((c * LB + r) * T, T), T)

    def load(c, a):
        hbm, vmem = pairs_in[a]
        return pltpu.make_async_copy(hbm.at[:, cols(c)], vmem.at[:, cols(c)], in_sem.at[a, c])

    for c in range(NCH):
        for a in range(3):
            load(c, a).start()
    for c in range(NCH):
        load(c, 3).start()

    start = cx * T
    e0 = len_ref[0, 0]
    e1 = e0 + len_ref[0, 1]

    def seg(pos):
        return (pos >= e0).astype(I32) + (pos >= e1).astype(I32)

    m = iota(1)

    def same(i, which):
        own = seg(start + i)
        if which == 0:
            return own == seg(start + m)
        pos = start + which * T + m
        return (own == seg(pos)) & (pos >= 0) & (pos < 4 * T)

    i = iota(0)
    wmask[:, :T] = ((m > i) & same(i, -1)).astype(BF)
    wmask[:, T:] = ((m <= i) & same(i, 0)).astype(BF)
    vmask[:, :T] = ((m >= i) & same(i, 0)).astype(BF)
    vmask[:, T:] = ((m < i) & same(i, 1)).astype(BF)
    f = T - 1 - i
    hmask[...] = (((m > f) & same(f, -1)) | ((m <= f) & same(f, 0))).astype(F32)
    hot = (i == off_ref[...]).astype(F32)
    place[...] = hot.astype(BF)
    fetch[...] = hot.T.astype(BF)
    mirror = ((i + m == 0) | (i + m == T)).astype(BF)
    flip = (i + m == T - 1).astype(BF)
    own_side = i + m <= T - 1
    tb = taps_ref[...].astype(BF)
    taps[...] = tb.astype(F32)
    rtaps[...] = dot(tb, mirror)

    def part(buf, c, axis, dev):
        d, x = dev
        if axis == "x":
            return buf.at[c, :, :, :, x]
        if axis == "y":
            return buf.at[c, :, lax.rem(d // 2, 4)]
        return buf.at[c, d // 8, :, lax.rem(d, 2)]

    def moves(bufs, sems, orders, c, ph):
        axis = orders[c][ph]
        src, dst = bufs[ph], bufs[ph + 1]
        copies = [
            pltpu.make_async_copy(
                part(src, c, axis, me), part(dst, c, axis, me), sems[2].at[c, ph]
            )
        ]
        for n, peer in enumerate(peers[axis]):
            copies.append(
                pltpu.make_async_remote_copy(
                    src_ref=part(src, c, axis, peer),
                    dst_ref=part(dst, c, axis, me),
                    send_sem=sems[0].at[c, ph, n],
                    recv_sem=sems[1].at[c, ph, n],
                    device_id=peer,
                    device_id_type=MESH,
                )
            )
        return copies

    def begin(copies):
        for copy in copies:
            copy.start()

    def finish(copies):
        for copy in copies:
            copy.wait()

    there = ((fa, fb, fc, fd), (fs, fr, fl), ORDERS_THERE)
    back_way = ((ba, bb, bc, bd), (bs, br, bl), ORDERS_BACK)

    def rows16(value):
        return value.reshape(GRID + (16, T))

    def prep(c):
        for a in range(3):
            load(c, a).wait()
        for r in range(LB):
            at = block_of(c, r)
            sc[:, r, :] = qv[:, at].astype(F32)
            sc[:, LB + r, :] = kv[:, at].astype(F32) * vv[:, at].astype(F32)
        fa[c] = rows16(sc[...].astype(BF))

    def plan(c):
        load(c, 3).wait()
        sc[...] = fd[c].reshape(T, 16, T).astype(F32)
        for r in range(LB):
            both = jnp.concatenate([sc[:, r, :], sc[:, LB + r, :]], axis=1).astype(BF)
            planned = dot(place[...], both)
            qp[c, :, lanes(r)] = planned[:, :T].astype(BF)
            up[c, :, lanes(r)] = planned[:, T:].astype(BF)
            grad = gv[:, block_of(c, r)].astype(F32)
            inn[c, :, lanes(r)] = (grad * planned[:, :T]).astype(BF)

    def halo(c):
        copies = []
        for n, (src, dst, to) in enumerate(((up, ear, 0), (inn, lat, 1))):
            copy = pltpu.make_async_remote_copy(
                src_ref=src.at[c],
                dst_ref=dst.at[c],
                send_sem=hs.at[c, n],
                recv_sem=hr.at[c, n],
                device_id=peers["x"][to],
                device_id_type=MESH,
            )
            copies.append(copy)
        return copies

    lane_group = iota(1, (1, T)) // 16

    def make(n, slot):
        rows = pl.ds(pl.multiple_of(n * 8, 8), 8)
        t = taps[rows]
        rt = rtaps[rows]
        for g in range(8):
            back = jnp.broadcast_to(rt[g : g + 1], (T, T))
            back = pltpu.roll(back, 0, 1, stride=1, stride_axis=0).astype(BF)
            ahead = jnp.broadcast_to(t[g : g + 1], (T, T))
            ahead = pltpu.roll(ahead, 0, 1, stride=1, stride_axis=0).astype(BF)
            w_sc[slot, lanes(g)] = jnp.concatenate([back, back], axis=1) * wmask[...]
            v_sc[slot, lanes(g)] = jnp.concatenate([ahead, ahead], axis=1) * vmask[...]

    def use(c, n, slot):
        at = pl.ds(pl.multiple_of(n * T, T), T)
        full = pl.ds(pl.multiple_of((c * LB + n) * T, T), T)
        u = up[c, :, at]
        inner_b = inn[c, :, at]
        u2 = jnp.concatenate([ear[c, :, at], u], axis=0)
        i2 = jnp.concatenate([inner_b, lat[c, :, at]], axis=0)
        f_all = dot(w_sc[slot], u2)
        d_all = dot(v_sc[slot], i2)
        turned = dot(flip, inner_b).astype(BF)
        zero = jnp.zeros((), BF)
        mine = jnp.concatenate([jnp.where(lane_group == g, turned, zero) for g in range(8)], axis=0)
        pairs = dot(mine, u2, ((1,), (1,)))
        f, d = f_all[:T], d_all[:T]
        lags = []
        for g in range(8):
            if g:
                f = jnp.where(lane_group == g, f_all[lanes(g)], f)
                d = jnp.where(lane_group == g, d_all[lanes(g)], d)
            p = pairs[lanes(g)]
            p = jnp.where(own_side, p[:, T:], p[:, :T]) * hmask[...]
            p = pltpu.roll(p, 1, 1, stride=1, stride_axis=0)
            lags.append(jnp.sum(p, axis=0, keepdims=True))
        gain = gain_ref[:, full]
        uf = u.astype(F32)
        qf = qp[c, :, at].astype(F32)
        gf = gv[:, full].astype(F32)
        inner = gf * qf
        gated = f + gain * uf
        gv[:, full] = (qf * gated).astype(BF)
        dq_sc[:, at] = (gf * gated).astype(BF)
        du_sc[:, at] = (d + gain * inner).astype(BF)
        skip = jnp.sum(inner * uf, axis=0, keepdims=True)
        other = pltpu.roll(skip, T // 2, 1)
        pad = jnp.zeros((3, T), F32)
        block = c * LB + n
        term[2 * block] = jnp.concatenate(lags[:4] + [skip, pad], axis=0)
        term[2 * block + 1] = jnp.concatenate(lags[4:] + [other, pad], axis=0)

    def conv(c):
        def step(j, carry):
            block = c * LB + 2 * j
            use(c, 2 * j, 0)
            make(block + 1, 1)
            use(c, 2 * j + 1, 1)
            make(lax.rem(block + 2, NCH * LB), 0)
            return carry

        lax.fori_loop(0, LB // 2, step, 0)
        for r in range(LB):
            both = jnp.concatenate([dq_sc[:, lanes(r)], du_sc[:, lanes(r)]], axis=1)
            back = dot(fetch[...], both)
            sc[:, r, :] = back[:, :T]
            sc[:, LB + r, :] = back[:, T:]
        ba[c] = rows16(sc[...].astype(BF))

    def store(c, a):
        vmem, hbm = ((gv, out_hbm), (qv, qg_hbm), (kv, kg_hbm), (vv, vg_hbm))[a]
        return pltpu.make_async_copy(vmem.at[:, cols(c)], hbm.at[:, cols(c)], out_sem.at[a, c])

    def last(c):
        sc[...] = bd[c].reshape(T, 16, T).astype(F32)
        for r in range(LB):
            at = block_of(c, r)
            qv[:, at] = sc[:, r, :].astype(BF)
            du = sc[:, LB + r, :]
            kf = kv[:, at].astype(F32)
            vf = vv[:, at].astype(F32)
            kv[:, at] = (du * vf).astype(BF)
            vv[:, at] = (du * kf).astype(BF)
        for a in (1, 2, 3):
            store(c, a).start()

    grid = term.reshape(GRID + (8, T))

    def term_moves(axis):
        view, slots, base = {
            "x": (lambda p: grid.at[:, :, :, p[1]], rx, 0),
            "y": (lambda p: s1.at[:, lax.rem(p[0] // 2, 4)], ry, 3),
            "z": (lambda p: s2.at[p[0] // 8, lax.rem(p[0], 2)], rz, 6),
        }[axis]
        return [
            pltpu.make_async_remote_copy(
                src_ref=view(peer), dst_ref=slots.at[n], send_sem=rs.at[base + n],
                recv_sem=rr.at[base + n], device_id=peer, device_id_type=MESH,
            )
            for n, peer in enumerate(peers[axis])
        ]

    def reduce(stage):
        if stage == 0:
            begin(term_moves("x"))
        elif stage == 1:
            finish(term_moves("x"))
            s1[...] = grid[:, :, :, cx] + rx[0] + rx[1] + rx[2]
            begin(term_moves("y"))
        elif stage == 2:
            finish(term_moves("y"))
            s2[...] = s1[:, y] + ry[0] + ry[1] + ry[2]
            begin(term_moves("z"))
        else:
            finish(term_moves("z"))
            total = s2[z, k]
            for n in range(7):
                total = total + rz[n]
            hi = total.astype(BF)
            rest = total - hi.astype(F32)
            mid = rest.astype(BF)
            low = (rest - mid.astype(F32)).astype(BF)
            turned = dot(hi, mirror) + dot(mid, mirror) + dot(low, mirror)
            row = iota(0, (8, T))
            tokens = T * T
            sum_ref[...] = jnp.where(
                row < 4, turned * (1 / math.sqrt(tokens * 16)), total * (1 / math.sqrt(tokens))
            )

    def move(code):
        kind, c, ph = code // 100, code // 10 % 10, code % 10
        if kind == MOVE_TERMS:
            reduce(ph)
            return
        way = there if kind == MOVE_THERE else back_way
        if ph:
            finish(moves(*way, c, ph - 1))
        if ph < 3:
            begin(moves(*way, c, ph))

    def work(kind, c):
        if kind == PREP:
            prep(c)
        elif kind == PLAN:
            plan(c)
            begin(halo(c))
        elif kind == CONV:
            finish(halo(c))
            conv(c)
            store(c, 0).start()
        else:
            last(c)

    steps = [([], None)]
    for code in SCHEDULE:
        if code < 400:
            steps[-1] = (steps[-1][0], code // 100)
            steps.append(([], None))
        else:
            steps[-1][0].append(code)
    tail = steps.pop()[0]

    def choose(i, low, high):
        if not any(steps[n][0] for n in range(low, high)):
            return
        if high - low == 1:
            for code in steps[low][0]:
                move(code)
            return
        mid = (low + high) // 2
        pl.when(i < mid)(lambda: choose(i, low, mid))
        pl.when(i >= mid)(lambda: choose(i, mid, high))

    words = [
        sum(steps[n][1] << (2 * (n - first)) for n in range(first, min(first + 12, len(steps))))
        for first in range(0, len(steps), 12)
    ]

    def step(i, counts):
        choose(i, 0, len(steps))
        word = jnp.asarray(words[0], I32)
        for n in range(1, len(words)):
            word = jnp.where(i >= 12 * n, words[n], word)
        kind = lax.rem(lax.shift_right_logical(word, 2 * lax.rem(i, 12)), 4)
        for n in range(4):
            pl.when(kind == n)(lambda n=n: work(n, counts[n]))
        return tuple(counts[n] + (kind == n).astype(I32) for n in range(4))

    pl.semaphore_wait(barrier, sum(len(peers[axis]) for axis in "xyz"))
    make(0, 0)
    zero_count = jnp.zeros((), I32)
    lax.fori_loop(0, len(steps), step, (zero_count,) * 4)
    for code in tail:
        move(code)
    for c in range(NCH):
        for a in range(4):
            store(c, a).wait()


def body(q_rows, k_rows, v_rows, out_grad, filters, skip_gain, genome_len, plan_offset):
    chans = q_rows.shape[1]
    wide = (T, chans)
    act = jax.ShapeDtypeStruct(wide, BF)
    anywhere = pl.BlockSpec(memory_space=pl.ANY)
    vmem = pl.BlockSpec(memory_space=pltpu.VMEM)
    smem = pl.BlockSpec(memory_space=pltpu.SMEM)
    flow = pltpu.VMEM((NCH,) + GRID + (16, T), BF)
    chunked = pltpu.VMEM((NCH, T, WIDE), BF)
    dma = pltpu.SemaphoreType.DMA
    groups = filters.shape[0]
    *outs, sums = pl.pallas_call(
        mixer_kernel,
        in_specs=[anywhere] * 4 + [vmem, vmem, smem, vmem],
        out_specs=[anywhere] * 4 + [vmem],
        out_shape=[act] * 4 + [jax.ShapeDtypeStruct((8, T), F32)],
        scratch_shapes=[pltpu.VMEM(wide, BF)] * 4
        + [flow] * 8
        + [chunked] * 5
        + [
            pltpu.VMEM((T, 2 * T), BF),
            pltpu.VMEM((T, 2 * T), BF),
            pltpu.VMEM((T, T), F32),
            pltpu.VMEM((T, T), BF),
            pltpu.VMEM((T, T), BF),
            pltpu.VMEM((groups, T), F32),
            pltpu.VMEM((groups, T), F32),
            pltpu.VMEM((2, 8 * T, 2 * T), BF),
            pltpu.VMEM((2, 8 * T, 2 * T), BF),
            pltpu.VMEM((T, 16, T), F32),
            pltpu.VMEM((T, WIDE), BF),
            pltpu.VMEM((T, WIDE), BF),
            pltpu.VMEM((T, 8, T), F32),
            pltpu.VMEM((3, 4, 4, 2, 8, T), F32),
            pltpu.VMEM((3, 4, 2, 8, T), F32),
            pltpu.VMEM((7, 8, T), F32),
            pltpu.VMEM((4, 4, 2, 8, T), F32),
            pltpu.VMEM((4, 2, 8, T), F32),
            dma((4, NCH)),
            dma((4, NCH)),
            dma((NCH, 3, 7)),
            dma((NCH, 3, 7)),
            dma((NCH, 3)),
            dma((NCH, 3, 7)),
            dma((NCH, 3, 7)),
            dma((NCH, 3)),
            dma((NCH, 2)),
            dma((NCH, 2)),
            dma((13,)),
            dma((13,)),
        ],
        compiler_params=pltpu.CompilerParams(
            collective_id=0, has_side_effects=True, vmem_limit_bytes=60 * 2**20
        ),
        name="mixer",
    )(
        q_rows, k_rows, v_rows, out_grad, filters, skip_gain.reshape(1, chans), genome_len,
        plan_offset.reshape(1, T),
    )
    return (*outs, sums[:4], sums[4, : chans // T])


def solution(mesh):
    rows = P(("dp", "ctx"), None)
    return jax.shard_map(
        body,
        mesh=mesh,
        in_specs=(rows, rows, rows, rows, P(), P(), P("dp", None), P(None, ("dp", "ctx"), None)),
        out_specs=(rows, rows, rows, rows, rows, P(("dp", "ctx"))),
        check_vma=False,
    )
```

profile of v0, /device:TPU:1, one launch (start us, length us, event | category | flops | bytes accessed | tf_op | source)
XLA Modules:
  0.0 174.4 jit_solution(17001653728689432587)
XLA Ops:
  0.6 162.0 %mixer.1 = (bf16[128,8192]{1,0:T(8,128)(2,1)}, bf16[128,8192]{1,0:T(8,128)(2,1)}, bf16[128,8192]{1,0:T(8,128)(2,1)}, bf16[128,8192]{1,0:T(8,128)(2,1)}, f32[8,128]{1,0:T(8,128)}) custom-call(bf16[128,8192]{1,0:T(8,128)(2,1)} %q_hbm.1, bf16[128,8192]{1,0:T(8,128)(2,1)} %k_hbm.1, bf16[128,8192]{1,0:T(8,128)(2,1)} %v_hbm.1, bf16[128,8192]{1,0:T(8,128)(2,1)} %g_hbm.1, ...), custom_call_target="tpu_custom_call" | custom-call | tf_op jit(solution)/shard_map/mixer/pallas_call | solution.py:408
  162.7 1.3 slice.6
  163.9 1.2 slice_bitcast_fusion
  165.1 0.0 copy-start.2
  165.1 3.2 %copy.18 = bf16[128,8192]{1,0:T(8,128)(2,1)} copy(bf16[128,8192]{1,0:T(8,128)(2,1)} %get-tuple-element.22) | data formatting | bytes 4194304
  168.3 0.0 copy-done.2
  168.4 0.0 copy-start.1
  168.4 1.3 copy.19
  169.7 1.0 copy-done.1
  170.7 0.0 copy-start
  170.7 1.3 copy.20
  172.0 1.0 copy-done
  173.0 1.3 copy.21
Async XLA Ops:
  165.1 3.2 %copy-start.2 = (bf16[128,8192]{1,0:T(8,128)(2,1)S(1)}, bf16[128,8192]{1,0:T(8,128)(2,1)}, u32[]{:S(2)}) copy-start(bf16[128,8192]{1,0:T(8,128)(2,1)} %get-tuple-element.23) | copy-start | bytes 6291460
  168.4 2.3 %copy-start.1 = (bf16[128,8192]{1,0:T(8,128)(2,1)S(1)}, bf16[128,8192]{1,0:T(8,128)(2,1)}, u32[]{:S(2)}) copy-start(bf16[128,8192]{1,0:T(8,128)(2,1)} %get-tuple-element.24) | copy-start | bytes 6291460
  170.7 2.3 %copy-start = (bf16[128,8192]{1,0:T(8,128)(2,1)S(1)}, bf16[128,8192]{1,0:T(8,128)(2,1)}, u32[]{:S(2)}) copy-start(bf16[128,8192]{1,0:T(8,128)(2,1)} %get-tuple-element.25) | copy-start | bytes 6291460
where the time goes:
time: 176 us; the launch traced here: 174 us
  Pallas kernels  162 us (92%)
  local copies, waits for them, and re-layouts  11.7 us (7%)
    pallas_call x1, Pallas kernels, body(): pl.pallas_call(mixer_kernel, in_specs=[anywhere] * 4 + [vmem, vmem, smem,...  162 us
    unnamed x10, local copies, waits for them, and re-layouts  9.26 us

commit v1 on v0

--- a/solution.py
+++ b/solution.py
@@ -16,16 +16,16 @@
 LB = 8
 WIDE = LB * T
 GRID = (4, 4, 2, 4)
-PREP, PLAN, CONV, LAST, MOVE_THERE, MOVE_BACK, MOVE_TERMS = range(7)
+PREP, PLAN, CONV, LAST, MOVE_THERE, MOVE_BACK, MOVE_TERMS, SET_UP = range(8)
 ORDERS_THERE = ("xzy", "yxz", "yzx", "xyz", "xzy", "xyz", "yxz", "yxz")
 ORDERS_BACK = ("zyx", "zxy", "zxy", "zyx", "yzx", "zyx", "zxy", "zyx")
 SCHEDULE = (
-    0, 400, 0, 410, 0, 420, 0, 430, 401, 411, 0, 440, 0, 450, 421, 431, 402, 0, 460, 412, 422,
-    441, 432, 451, 403, 100, 442, 0, 470, 461, 413, 100, 423, 100, 452, 200, 500, 433, 100, 471,
-    443, 100, 200, 510, 501, 453, 100, 462, 200, 520, 200, 530, 463, 100, 472, 502, 200, 540, 521,
-    200, 550, 531, 473, 100, 200, 560, 511, 551, 532, 522, 541, 200, 570, 600, 561, 503, 300, 601,
-    512, 552, 602, 542, 571, 603, 513, 300, 523, 300, 533, 300, 562, 572, 543, 300, 553, 300, 563,
-    300, 573, 300,
+    0, 400, 0, 410, 0, 420, 700, 0, 430, 401, 411, 0, 440, 0, 450, 421, 431, 402, 0, 460, 412,
+    422, 441, 432, 451, 403, 100, 442, 0, 470, 461, 413, 100, 423, 100, 452, 200, 500, 433, 100,
+    471, 443, 100, 200, 510, 501, 453, 100, 462, 200, 520, 200, 530, 463, 100, 472, 502, 200, 540,
+    521, 200, 550, 531, 473, 100, 200, 560, 511, 551, 532, 522, 541, 200, 570, 600, 561, 503, 300,
+    601, 512, 552, 602, 542, 571, 603, 513, 300, 523, 300, 533, 300, 562, 572, 543, 300, 553, 300,
+    563, 300, 573, 300,
 )
 
 
@@ -43,11 +43,11 @@
 
 def mixer_kernel(
     q_hbm, k_hbm, v_hbm, g_hbm, taps_ref, gain_ref, len_ref, off_ref,
-    out_hbm, qg_hbm, kg_hbm, vg_hbm, sum_ref,
-    qv, kv, vv, gv, fa, fb, fc, fd, ba, bb, bc, bd, qp, up, ear, inn, lat,
+    gv, qv, kv, vv, filter_ref, skip_ref,
+    fa, fb, fc, fd, ba, bb, bc, bd, qp, up, ear, inn, lat,
     wmask, vmask, hmask, place, fetch, taps, rtaps, w_sc, v_sc, sc, dq_sc, du_sc,
     term, rx, ry, rz, s1, s2,
-    in_sem, out_sem, fs, fr, fl, bs, br, bl, hs, hr, rs, rr,
+    in_sem, fs, fr, fl, bs, br, bl, hs, hr, rs, rr,
 ):
     dp = lax.axis_index("dp")
     cx = lax.axis_index("ctx")
@@ -84,38 +84,39 @@
     for c in range(NCH):
         load(c, 3).start()
 
-    start = cx * T
-    e0 = len_ref[0, 0]
-    e1 = e0 + len_ref[0, 1]
-
-    def seg(pos):
-        return (pos >= e0).astype(I32) + (pos >= e1).astype(I32)
-
+    i = iota(0)
     m = iota(1)
-
-    def same(i, which):
-        own = seg(start + i)
-        if which == 0:
-            return own == seg(start + m)
-        pos = start + which * T + m
-        return (own == seg(pos)) & (pos >= 0) & (pos < 4 * T)
-
-    i = iota(0)
-    wmask[:, :T] = ((m > i) & same(i, -1)).astype(BF)
-    wmask[:, T:] = ((m <= i) & same(i, 0)).astype(BF)
-    vmask[:, :T] = ((m >= i) & same(i, 0)).astype(BF)
-    vmask[:, T:] = ((m < i) & same(i, 1)).astype(BF)
-    f = T - 1 - i
-    hmask[...] = (((m > f) & same(f, -1)) | ((m <= f) & same(f, 0))).astype(F32)
-    hot = (i == off_ref[...]).astype(F32)
-    place[...] = hot.astype(BF)
-    fetch[...] = hot.T.astype(BF)
     mirror = ((i + m == 0) | (i + m == T)).astype(BF)
     flip = (i + m == T - 1).astype(BF)
     own_side = i + m <= T - 1
-    tb = taps_ref[...].astype(BF)
-    taps[...] = tb.astype(F32)
-    rtaps[...] = dot(tb, mirror)
+
+    def set_up():
+        start = cx * T
+        e0 = len_ref[0, 0]
+        e1 = e0 + len_ref[0, 1]
+
+        def seg(pos):
+            return (pos >= e0).astype(I32) + (pos >= e1).astype(I32)
+
+        def same(i, which):
+            own = seg(start + i)
+            if which == 0:
+                return own == seg(start + m)
+            pos = start + which * T + m
+            return (own == seg(pos)) & (pos >= 0) & (pos < 4 * T)
+
+        wmask[:, :T] = ((m > i) & same(i, -1)).astype(BF)
+        wmask[:, T:] = ((m <= i) & same(i, 0)).astype(BF)
+        vmask[:, :T] = ((m >= i) & same(i, 0)).astype(BF)
+        vmask[:, T:] = ((m < i) & same(i, 1)).astype(BF)
+        f = T - 1 - i
+        hmask[...] = (((m > f) & same(f, -1)) | ((m <= f) & same(f, 0))).astype(F32)
+        hot = (i == off_ref[...]).astype(F32)
+        place[...] = hot.astype(BF)
+        fetch[...] = hot.T.astype(BF)
+        tb = taps_ref[...].astype(BF)
+        taps[...] = tb.astype(F32)
+        rtaps[...] = dot(tb, mirror)
 
     def part(buf, c, axis, dev):
         d, x = dev
@@ -264,10 +265,6 @@
             sc[:, LB + r, :] = back[:, T:]
         ba[c] = rows16(sc[...].astype(BF))
 
-    def store(c, a):
-        vmem, hbm = ((gv, out_hbm), (qv, qg_hbm), (kv, kg_hbm), (vv, vg_hbm))[a]
-        return pltpu.make_async_copy(vmem.at[:, cols(c)], hbm.at[:, cols(c)], out_sem.at[a, c])
-
     def last(c):
         sc[...] = bd[c].reshape(T, 16, T).astype(F32)
         for r in range(LB):
@@ -278,16 +275,14 @@
             vf = vv[:, at].astype(F32)
             kv[:, at] = (du * vf).astype(BF)
             vv[:, at] = (du * kf).astype(BF)
-        for a in (1, 2, 3):
-            store(c, a).start()
 
     grid = term.reshape(GRID + (8, T))
 
     def term_moves(axis):
         view, slots, base = {
-            "x": (lambda p: grid.at[:, :, :, p[1]], rx, 0),
-            "y": (lambda p: s1.at[:, lax.rem(p[0] // 2, 4)], ry, 3),
-            "z": (lambda p: s2.at[p[0] // 8, lax.rem(p[0], 2)], rz, 6),
+            "y": (lambda p: grid.at[:, lax.rem(p[0] // 2, 4)], ry, 0),
+            "z": (lambda p: s1.at[p[0] // 8, lax.rem(p[0], 2)], rz, 3),
+            "x": (lambda p: s2.at[p[1]], rx, 10),
         }[axis]
         return [
             pltpu.make_async_remote_copy(
@@ -299,33 +294,36 @@
 
     def reduce(stage):
         if stage == 0:
-            begin(term_moves("x"))
+            begin(term_moves("y"))
         elif stage == 1:
-            finish(term_moves("x"))
-            s1[...] = grid[:, :, :, cx] + rx[0] + rx[1] + rx[2]
-            begin(term_moves("y"))
+            finish(term_moves("y"))
+            s1[...] = grid[:, y] + ry[0] + ry[1] + ry[2]
+            begin(term_moves("z"))
         elif stage == 2:
-            finish(term_moves("y"))
-            s2[...] = s1[:, y] + ry[0] + ry[1] + ry[2]
-            begin(term_moves("z"))
-        else:
             finish(term_moves("z"))
-            total = s2[z, k]
+            total = s1[z, k]
             for n in range(7):
                 total = total + rz[n]
+            s2[...] = total
+            begin(term_moves("x"))
+        else:
+            finish(term_moves("x"))
+            total = s2[cx] + rx[0] + rx[1] + rx[2]
             hi = total.astype(BF)
             rest = total - hi.astype(F32)
             mid = rest.astype(BF)
             low = (rest - mid.astype(F32)).astype(BF)
             turned = dot(hi, mirror) + dot(mid, mirror) + dot(low, mirror)
-            row = iota(0, (8, T))
             tokens = T * T
-            sum_ref[...] = jnp.where(
-                row < 4, turned * (1 / math.sqrt(tokens * 16)), total * (1 / math.sqrt(tokens))
-            )
+            filter_ref[...] = turned[:4] * (1 / math.sqrt(tokens * 16))
+            skip_ref[...] = total[4:5, :64] * (1 / math.sqrt(tokens))
 
     def move(code):
         kind, c, ph = code // 100, code // 10 % 10, code % 10
+        if kind == SET_UP:
+            set_up()
+            make(0, 0)
+            return
         if kind == MOVE_TERMS:
             reduce(ph)
             return
@@ -344,7 +342,6 @@
         elif kind == CONV:
             finish(halo(c))
             conv(c)
-            store(c, 0).start()
         else:
             last(c)
 
@@ -384,20 +381,16 @@
         return tuple(counts[n] + (kind == n).astype(I32) for n in range(4))
 
     pl.semaphore_wait(barrier, sum(len(peers[axis]) for axis in "xyz"))
-    make(0, 0)
     zero_count = jnp.zeros((), I32)
     lax.fori_loop(0, len(steps), step, (zero_count,) * 4)
     for code in tail:
         move(code)
-    for c in range(NCH):
-        for a in range(4):
-            store(c, a).wait()
 
 
 def body(q_rows, k_rows, v_rows, out_grad, filters, skip_gain, genome_len, plan_offset):
     chans = q_rows.shape[1]
     wide = (T, chans)
-    act = jax.ShapeDtypeStruct(wide, BF)
+    act = pltpu.VMEM(wide, BF)
     anywhere = pl.BlockSpec(memory_space=pl.ANY)
     vmem = pl.BlockSpec(memory_space=pltpu.VMEM)
     smem = pl.BlockSpec(memory_space=pltpu.SMEM)
@@ -405,13 +398,16 @@
     chunked = pltpu.VMEM((NCH, T, WIDE), BF)
     dma = pltpu.SemaphoreType.DMA
     groups = filters.shape[0]
-    *outs, sums = pl.pallas_call(
+    *outs, filter_grad, skip_grad = pl.pallas_call(
         mixer_kernel,
         in_specs=[anywhere] * 4 + [vmem, vmem, smem, vmem],
-        out_specs=[anywhere] * 4 + [vmem],
-        out_shape=[act] * 4 + [jax.ShapeDtypeStruct((8, T), F32)],
-        scratch_shapes=[pltpu.VMEM(wide, BF)] * 4
-        + [flow] * 8
+        out_specs=[vmem] * 6,
+        out_shape=[act] * 4
+        + [
+            jax.ShapeDtypeStruct((groups // T, T), F32),
+            jax.ShapeDtypeStruct((1, chans // T), F32),
+        ],
+        scratch_shapes=[flow] * 8
         + [chunked] * 5
         + [
             pltpu.VMEM((T, 2 * T), BF),
@@ -427,12 +423,11 @@
             pltpu.VMEM((T, WIDE), BF),
             pltpu.VMEM((T, WIDE), BF),
             pltpu.VMEM((T, 8, T), F32),
-            pltpu.VMEM((3, 4, 4, 2, 8, T), F32),
-            pltpu.VMEM((3, 4, 2, 8, T), F32),
-            pltpu.VMEM((7, 8, T), F32),
-            pltpu.VMEM((4, 4, 2, 8, T), F32),
-            pltpu.VMEM((4, 2, 8, T), F32),
-            dma((4, NCH)),
+            pltpu.VMEM((3, 8, T), F32),
+            pltpu.VMEM((3, 4, 2, 4, 8, T), F32),
+            pltpu.VMEM((7, 4, 8, T), F32),
+            pltpu.VMEM((4, 2, 4, 8, T), F32),
+            pltpu.VMEM((4, 8, T), F32),
             dma((4, NCH)),
             dma((NCH, 3, 7)),
             dma((NCH, 3, 7)),
@@ -446,14 +441,14 @@
             dma((13,)),
         ],
         compiler_params=pltpu.CompilerParams(
-            collective_id=0, has_side_effects=True, vmem_limit_bytes=60 * 2**20
+            collective_id=0, has_side_effects=True, vmem_limit_bytes=52 * 2**20
         ),
         name="mixer",
     )(
         q_rows, k_rows, v_rows, out_grad, filters, skip_gain.reshape(1, chans), genome_len,
         plan_offset.reshape(1, T),
     )
-    return (*outs, sums[:4], sums[4, : chans // T])
+    return (*outs, filter_grad, skip_grad.reshape(chans // T))
 
 
 def solution(mesh):

time: 176 us -> 166 us (0.943)
  local copies, waits for them, and re-layouts: 11.7 us -> 6.37 us
  Pallas kernels: 162 us -> 158 us
    pallas_call x1, Pallas kernels: 162 us -> 158 us  [body(): pl.pallas_call(mixer_kernel, in_specs=[anywhere] * 4 + [vmem, vmem, smem,...]
    unnamed x10, local copies, waits for them, and re-layouts: 9.26 us -> 6.37 us
where the time goes in v1:
time: 166 us; the launch traced here: 165 us
  Pallas kernels  158 us (95%)
  local copies, waits for them, and re-layouts  6.37 us (4%)
    pallas_call x1, Pallas kernels, body(): pl.pallas_call(mixer_kernel, in_specs=[anywhere] * 4 + [vmem, vmem, smem,...  158 us
    unnamed x10, local copies, waits for them, and re-layouts  6.37 us

profile of v1, /device:TPU:1, one launch (start us, length us, event | category | flops | bytes accessed | tf_op | source)
XLA Modules:
  0.0 164.9 jit_solution(9279614542151253105)
XLA Ops:
  0.6 157.9 %mixer.1 = (bf16[128,8192]{1,0:T(8,128)(2,1)S(1)}, bf16[128,8192]{1,0:T(8,128)(2,1)S(1)}, bf16[128,8192]{1,0:T(8,128)(2,1)S(1)}, bf16[128,8192]{1,0:T(8,128)(2,1...) custom-call(bf16[128,8192]{1,0:T(8,128)(2,1)} %q_hbm.1, bf16[128,8192]{1,0:T(8,128)(2,1)} %k_hbm.1, bf16[128,8192]{1,0:T(8,128)(2,1)} %v_hbm.1, ...), custom_call_target="tpu_custom_call" | custom-call | tf_op jit(solution)/shard_map/mixer/pallas_call | solution.py:401
  158.5 1.3 copy.20
  159.9 1.3 copy.21
  161.2 1.3 copy.22
  162.5 0.0 copy-start
  162.5 0.0 copy-start.1
  162.5 1.3 copy.23
  163.8 0.0 copy-done
  163.8 0.6 copy.24
  164.4 0.0 copy-done.1
  164.4 0.5 copy.25
Async XLA Ops:
  162.5 1.3 copy-start
  162.5 1.9 %copy-start.1 = (f32[1,64]{1,0:T(1,128)S(1)}, f32[1,64]{1,0:T(1,128)}, u32[]{:S(2)}) copy-start(f32[1,64]{1,0:T(1,128)} %get-tuple-element.17) | copy-start | bytes 772

commit v2 on v1

--- a/solution.py
+++ b/solution.py
@@ -20,12 +20,12 @@
 ORDERS_THERE = ("xzy", "yxz", "yzx", "xyz", "xzy", "xyz", "yxz", "yxz")
 ORDERS_BACK = ("zyx", "zxy", "zxy", "zyx", "yzx", "zyx", "zxy", "zyx")
 SCHEDULE = (
-    0, 400, 0, 410, 0, 420, 700, 0, 430, 401, 411, 0, 440, 0, 450, 421, 431, 402, 0, 460, 412,
-    422, 441, 432, 451, 403, 100, 442, 0, 470, 461, 413, 100, 423, 100, 452, 200, 500, 433, 100,
-    471, 443, 100, 200, 510, 501, 453, 100, 462, 200, 520, 200, 530, 463, 100, 472, 502, 200, 540,
-    521, 200, 550, 531, 473, 100, 200, 560, 511, 551, 532, 522, 541, 200, 570, 600, 561, 503, 300,
-    601, 512, 552, 602, 542, 571, 603, 513, 300, 523, 300, 533, 300, 562, 572, 543, 300, 553, 300,
-    563, 300, 573, 300,
+    0, 400, 700, 0, 410, 0, 420, 710, 0, 430, 401, 411, 0, 440, 0, 450, 421, 431, 402, 0, 460,
+    412, 422, 441, 432, 451, 403, 100, 442, 0, 470, 461, 413, 100, 423, 100, 452, 200, 500, 433,
+    100, 471, 443, 100, 200, 510, 501, 453, 100, 462, 200, 520, 200, 530, 463, 100, 472, 502, 200,
+    540, 521, 200, 550, 531, 473, 100, 200, 560, 511, 551, 532, 522, 541, 200, 570, 600, 561, 503,
+    300, 601, 512, 552, 602, 542, 571, 603, 513, 300, 523, 300, 533, 300, 562, 572, 543, 300, 553,
+    300, 563, 300, 573, 300,
 )
 
 
@@ -61,10 +61,6 @@
             for i, j in ((1, 0), (3, 0), (2, 0), (1, 1), (3, 1), (2, 1), (0, 1))
         ],
     }
-    barrier = pltpu.get_barrier_semaphore()
-    for axis in "xyz":
-        for peer in peers[axis]:
-            pl.semaphore_signal(barrier, inc=1, device_id=peer, device_id_type=MESH)
 
     pairs_in = ((q_hbm, qv), (k_hbm, kv), (v_hbm, vv), (g_hbm, gv))
 
@@ -78,11 +74,6 @@
         hbm, vmem = pairs_in[a]
         return pltpu.make_async_copy(hbm.at[:, cols(c)], vmem.at[:, cols(c)], in_sem.at[a, c])
 
-    for c in range(NCH):
-        for a in range(3):
-            load(c, a).start()
-    for c in range(NCH):
-        load(c, 3).start()
 
     i = iota(0)
     m = iota(1)
@@ -118,13 +109,29 @@
         taps[...] = tb.astype(F32)
         rtaps[...] = dot(tb, mirror)
 
+    for a in range(3):
+        load(0, a).start()
+    barrier = pltpu.get_barrier_semaphore()
+    for axis in "xyz":
+        for peer in peers[axis]:
+            pl.semaphore_signal(barrier, inc=1, device_id=peer, device_id_type=MESH)
+    for a in range(3):
+        load(1, a).start()
+
+    def load_rest():
+        for c in range(2, NCH):
+            for a in range(3):
+                load(c, a).start()
+        for c in range(NCH):
+            load(c, 3).start()
+
     def part(buf, c, axis, dev):
         d, x = dev
         if axis == "x":
-            return buf.at[c, :, :, :, x]
+            return buf.at[c, x]
         if axis == "y":
-            return buf.at[c, :, lax.rem(d // 2, 4)]
-        return buf.at[c, d // 8, :, lax.rem(d, 2)]
+            return buf.at[c, :, :, :, lax.rem(d // 2, 4)]
+        return buf.at[c, :, d // 8, lax.rem(d, 2)]
 
     def moves(bufs, sems, orders, c, ph):
         axis = orders[c][ph]
@@ -158,8 +165,17 @@
     there = ((fa, fb, fc, fd), (fs, fr, fl), ORDERS_THERE)
     back_way = ((ba, bb, bc, bd), (bs, br, bl), ORDERS_BACK)
 
-    def rows16(value):
-        return value.reshape(GRID + (16, T))
+    by_grid = sc.reshape(GRID + (16, T))
+
+    def pack(buf, c):
+        for k in range(2):
+            for x in range(4):
+                buf[c, x, :, k] = by_grid[:, :, k, x].astype(BF)
+
+    def unpack(buf, c):
+        for k in range(2):
+            for x in range(4):
+                by_grid[:, :, k, x] = buf[c, x, :, k].astype(F32)
 
     def prep(c):
         for a in range(3):
@@ -168,11 +184,11 @@
             at = block_of(c, r)
             sc[:, r, :] = qv[:, at].astype(F32)
             sc[:, LB + r, :] = kv[:, at].astype(F32) * vv[:, at].astype(F32)
-        fa[c] = rows16(sc[...].astype(BF))
+        pack(fa, c)
 
     def plan(c):
         load(c, 3).wait()
-        sc[...] = fd[c].reshape(T, 16, T).astype(F32)
+        unpack(fd, c)
         for r in range(LB):
             both = jnp.concatenate([sc[:, r, :], sc[:, LB + r, :]], axis=1).astype(BF)
             planned = dot(place[...], both)
@@ -263,10 +279,10 @@
             back = dot(fetch[...], both)
             sc[:, r, :] = back[:, :T]
             sc[:, LB + r, :] = back[:, T:]
-        ba[c] = rows16(sc[...].astype(BF))
+        pack(ba, c)
 
     def last(c):
-        sc[...] = bd[c].reshape(T, 16, T).astype(F32)
+        unpack(bd, c)
         for r in range(LB):
             at = block_of(c, r)
             qv[:, at] = sc[:, r, :].astype(BF)
@@ -320,6 +336,9 @@
 
     def move(code):
         kind, c, ph = code // 100, code // 10 % 10, code % 10
+        if kind == SET_UP and not c:
+            load_rest()
+            return
         if kind == SET_UP:
             set_up()
             make(0, 0)
@@ -387,6 +406,24 @@
         move(code)
 
 
+def hand_out(*refs):
+    n = 6
+    ins, outs, sems = refs[:n], refs[n : 2 * n], refs[-1]
+    copies = []
+    for a in range(4):
+        for part in range(4):
+            rows = pl.ds(part * 32, 32)
+            copies.append(
+                pltpu.make_async_copy(ins[a].at[rows], outs[a].at[rows], sems.at[a, part])
+            )
+    for copy in copies:
+        copy.start()
+    outs[4][...] = ins[4][...]
+    outs[5][...] = ins[5][...]
+    for copy in copies:
+        copy.wait()
+
+
 def body(q_rows, k_rows, v_rows, out_grad, filters, skip_gain, genome_len, plan_offset):
     chans = q_rows.shape[1]
     wide = (T, chans)
@@ -394,18 +431,18 @@
     anywhere = pl.BlockSpec(memory_space=pl.ANY)
     vmem = pl.BlockSpec(memory_space=pltpu.VMEM)
     smem = pl.BlockSpec(memory_space=pltpu.SMEM)
-    flow = pltpu.VMEM((NCH,) + GRID + (16, T), BF)
+    flow = pltpu.VMEM((NCH, 4, 4, 2, 4, 16, T), BF)
     chunked = pltpu.VMEM((NCH, T, WIDE), BF)
     dma = pltpu.SemaphoreType.DMA
     groups = filters.shape[0]
-    *outs, filter_grad, skip_grad = pl.pallas_call(
+    results = pl.pallas_call(
         mixer_kernel,
         in_specs=[anywhere] * 4 + [vmem, vmem, smem, vmem],
         out_specs=[vmem] * 6,
         out_shape=[act] * 4
         + [
-            jax.ShapeDtypeStruct((groups // T, T), F32),
-            jax.ShapeDtypeStruct((1, chans // T), F32),
+            pltpu.VMEM((groups // T, T), F32),
+            pltpu.VMEM((1, chans // T), F32),
         ],
         scratch_shapes=[flow] * 8
         + [chunked] * 5
@@ -448,7 +485,16 @@
         q_rows, k_rows, v_rows, out_grad, filters, skip_gain.reshape(1, chans), genome_len,
         plan_offset.reshape(1, T),
     )
-    return (*outs, filter_grad, skip_grad.reshape(chans // T))
+    *outs, skip_grad = pl.pallas_call(
+        hand_out,
+        in_specs=[vmem] * 6,
+        out_specs=[anywhere] * 4 + [vmem] * 2,
+        out_shape=[jax.ShapeDtypeStruct(r.shape, r.dtype) for r in results],
+        scratch_shapes=[dma((4, 4))],
+        compiler_params=pltpu.CompilerParams(vmem_limit_bytes=2 * 2**20),
+        name="hand_out",
+    )(*[pltpu.with_memory_space_constraint(r, pltpu.VMEM) for r in results])
+    return (*outs, skip_grad.reshape(chans // T))
 
 
 def solution(mesh):

time: 166 us -> 163 us (0.982)
  local copies, waits for them, and re-layouts: 6.37 us -> 0 us
  Pallas kernels: 158 us -> 162 us
    unnamed x10 -> x0, local copies, waits for them, and re-layouts: 6.37 us -> none
    pallas_call x0 -> x1, Pallas kernels: none -> 4 us  [body(): pl.pallas_call(hand_out, in_specs=[vmem] * 6, out_specs=[anywhere] * 4 +...]
where the time goes in v2:
time: 163 us; the launch traced here: 162 us
  Pallas kernels  162 us (99%)
    pallas_call x1, Pallas kernels, body(): pl.pallas_call(mixer_kernel, in_specs=[anywhere] * 4 + [vmem, vmem, smem,...  158 us
    pallas_call x1, Pallas kernels, body(): pl.pallas_call(hand_out, in_specs=[vmem] * 6, out_specs=[anywhere] * 4 +...  4 us

profile of v2, /device:TPU:1, one launch (start us, length us, event | category | flops | bytes accessed | tf_op | source)
XLA Modules:
  0.0 162.3 jit_solution(12328386334426253794)
XLA Ops:
  0.6 157.7 %mixer.1 = (bf16[128,8192]{1,0:T(8,128)(2,1)S(1)}, bf16[128,8192]{1,0:T(8,128)(2,1)S(1)}, bf16[128,8192]{1,0:T(8,128)(2,1)S(1)}, bf16[128,8192]{1,0:T(8,128)(2,1...) custom-call(bf16[128,8192]{1,0:T(8,128)(2,1)} %q_hbm.1, bf16[128,8192]{1,0:T(8,128)(2,1)} %k_hbm.1, ...), custom_call_target="tpu_custom_call" | custom-call | tf_op jit(solution)/shard_map/mixer/pallas_call | solution.py:438
  158.3 4.0 %hand_out.1 = (bf16[128,8192]{1,0:T(8,128)(2,1)}, bf16[128,8192]{1,0:T(8,128)(2,1)}, bf16[128,8192]{1,0:T(8,128)(2,1)}, bf16[128,8192]{1,0:T(8,128)(2,1)}, f32[4,128]{1,0:T(4,128)}, /*index=5*/f32[1,64]{1,0:T(1,128)}) custom-call(bf16[128,8192]{1,0:T(8,128)(2,1)S(1)} %get-tuple-element.18.refs_0_, bf16[128,8192]{1,0:T(8,128)(2,1)S(1)} %get-tuple-element.19.refs_1_, ...), custom_call_target="tpu_custom_call" | custom-call | tf_op jit(solution)/shard_map/hand_out/pallas_call | solution.py:488

commit v3 on v2

--- a/solution.py
+++ b/solution.py
@@ -54,11 +54,11 @@
     z, y, k = dp // 8, lax.rem(dp // 2, 4), lax.rem(dp, 2)
     me = (dp, cx)
     peers = {
-        "x": [(dp, lax.rem(cx + i, 4)) for i in (1, 3, 2)],
-        "y": [(z * 8 + lax.rem(y + i, 4) * 2 + k, cx) for i in (1, 3, 2)],
+        "x": [(dp, lax.rem(cx + i, 4)) for i in (2, 1, 3)],
+        "y": [(z * 8 + lax.rem(y + i, 4) * 2 + k, cx) for i in (2, 1, 3)],
         "z": [
             (lax.rem(z + i, 4) * 8 + y * 2 + lax.rem(k + j, 2), cx)
-            for i, j in ((1, 0), (3, 0), (2, 0), (1, 1), (3, 1), (2, 1), (0, 1))
+            for i, j in ((2, 0), (2, 1), (1, 0), (3, 0), (1, 1), (3, 1), (0, 1))
         ],
     }
 
@@ -199,7 +199,7 @@
 
     def halo(c):
         copies = []
-        for n, (src, dst, to) in enumerate(((up, ear, 0), (inn, lat, 1))):
+        for n, (src, dst, to) in enumerate(((up, ear, 1), (inn, lat, 2))):
             copy = pltpu.make_async_remote_copy(
                 src_ref=src.at[c],
                 dst_ref=dst.at[c],

time: 163 us -> 163 us (level)
  no operation moved by 1% of the time
where the time goes in v3:
time: 163 us
  Pallas kernels  163 us (100%)
    pallas_call x1, Pallas kernels, body(): pl.pallas_call(mixer_kernel, in_specs=[anywhere] * 4 + [vmem, vmem, smem,...  159 us
    pallas_call x1, Pallas kernels, body(): pl.pallas_call(hand_out, in_specs=[vmem] * 6, out_specs=[anywhere] * 4 +...  4 us

profile of v3, /device:TPU:1, one launch (start us, length us, event | category | flops | bytes accessed | tf_op | source)
XLA Modules:
  0.0 163.3 jit_solution(7253361935603854995)
XLA Ops:
  0.6 158.6 %mixer.1 = (bf16[128,8192]{1,0:T(8,128)(2,1)S(1)}, bf16[128,8192]{1,0:T(8,128)(2,1)S(1)}, bf16[128,8192]{1,0:T(8,128)(2,1)S(1)}, bf16[128,8192]{1,0:T(8,128)(2,1...) custom-call(bf16[128,8192]{1,0:T(8,128)(2,1)} %q_hbm.1, bf16[128,8192]{1,0:T(8,128)(2,1)} %k_hbm.1, ...), custom_call_target="tpu_custom_call" | custom-call | tf_op jit(solution)/shard_map/mixer/pallas_call | solution.py:438
  159.3 4.0 %hand_out.1 = (bf16[128,8192]{1,0:T(8,128)(2,1)}, bf16[128,8192]{1,0:T(8,128)(2,1)}, bf16[128,8192]{1,0:T(8,128)(2,1)}, bf16[128,8192]{1,0:T(8,128)(2,1)}, f32[4,128]{1,0:T(4,128)}, /*index=5*/f32[1,64]{1,0:T(1,128)}) custom-call(bf16[128,8192]{1,0:T(8,128)(2,1)S(1)} %get-tuple-element.18.refs_0_, bf16[128,8192]{1,0:T(8,128)(2,1)S(1)} %get-tuple-element.19.refs_1_, ...), custom_call_target="tpu_custom_call" | custom-call | tf_op jit(solution)/shard_map/hand_out/pallas_call | solution.py:488
